TPU v7x, 32 devices: a whole 2x2x4 slice. The times are simulated.
32 devices in a mesh: groups: 2 (over y), tx: 4 (over z), ty: 2 (over x), tz: 2 (over core).
Axes of the slice: x: 2, y: 2, z: 4, core: 2. Of those that a mesh axis runs over, the one named last changes fastest.
Arguments:
- phase: float32 [8, 64, 128, 256], P(None, ('groups', 'tx'), 'ty', 'tz'), parts along dimension 1, may hold values from 0 to 0.25
- slot_grain: int32 [8, 2, 2, 8], P(('groups', 'tx'), 'ty', 'tz'), parts along dimension 0, may hold values from 0 to 63, as said below
- crowding: int32 [8, 2, 2], P(('groups', 'tx'), 'ty', 'tz'), parts along dimension 0, may hold values from 4 to 8, as said below
- grain_home: int32 [128], P('groups'), parts along dimension 0, may hold values from 0 to 63, each once
- grain_weight: float32 [128], P('groups'), parts along dimension 0, may hold values from 0.5 to 2
- grain_target: float32 [128], P('groups'), parts along dimension 0, may hold values from 0.5 to 4
Outputs:
- phase_out: float32 [8, 64, 128, 256], P(None, ('groups', 'tx'), 'ty', 'tz'), parts along dimension 1
There are 2 independent parts, one for each index of `groups`. A program takes and returns all parts, laid end to end along the dimension named above; each array names one. Nothing has to cross between parts.
Inputs may be any that keep to these rules, and one draw needn't show every extreme that they name: `slot_grain`: within one tile the slots name distinct grains; tiles that share a face share grains. `crowding`: some tile has 8 live slots and some has 4.
All inputs are finite; a program needn't handle non-finite values.
Results may differ from a plain program's by a relative error of at most 0.0001.
Values sent between devices are 32-bit elements; how exact they have to be, the bound alone decides.
A program may use at most 64 MiB of HBM per device.

v0:
```python
import jax
import jax.numpy as jnp
from jax import lax
from jax.sharding import PartitionSpec as P

STEPS = 2


HIGH = lax.Precision.HIGHEST


def with_halo(block, sides, width):
    for axis, dim in sides:
        count = lax.axis_size(axis)
        forward = [(i, i + 1) for i in range(count - 1)]
        backward = [(target, source) for source, target in forward]
        low = lax.ppermute(
            lax.slice_in_dim(block, block.shape[dim] - width, None, axis=dim), axis, forward
        )
        high = lax.ppermute(lax.slice_in_dim(block, 0, width, axis=dim), axis, backward)
        block = jnp.concatenate([low, block, high], axis=dim)
    return block


def passed_along(block, axis, distance):
    devices = range(lax.axis_size(axis))
    route = [(i - distance, i) for i in devices if i - distance in devices]
    return lax.ppermute(block, axis, route)


def matched(mine, theirs_plus):
    same = (mine[:, None] + 1 == theirs_plus[None, :]) & (mine[:, None] >= 0)
    return same.astype(jnp.float32)


def remap(mapping, face):
    return jnp.einsum("ab,b...->a...", mapping, face, precision=HIGH)


def on_device(phase, slot_grain, crowding, grain_home, grain_weight, grain_target):
    slots = phase.shape[0]
    grains = grain_home.shape[0]
    cells = phase.shape[1] * phase.shape[2] * phase.shape[3]
    live = jnp.arange(slots) < crowding[0, 0, 0]
    slot_ids = jnp.where(live, slot_grain[0, 0, 0], -1)
    grain_hot = (slot_ids[:, None] == jnp.arange(grains)[None, :]).astype(jnp.float32)
    weights = jnp.dot(grain_hot, grain_weight, precision=HIGH)
    homes = jnp.sum(jnp.where(grain_hot > 0, grain_home[None, :], 0), axis=1)
    homes = jnp.where(live, homes, -1)
    home_hot = (homes[:, None] == jnp.arange(grains)[None, :]).astype(jnp.float32)
    neighbour_ids = with_halo(
        (slot_ids + 1).reshape(1, 1, 1, slots), (("tx", 0), ("ty", 1), ("tz", 2)), 1
    )
    plus_ids = slot_ids + 1
    weight_col = weights[:, None, None, None]
    phase = phase * live.astype(jnp.float32)[:, None, None, None]
    tile_sums = jnp.sum(phase, axis=(1, 2, 3))
    partial_volumes = jnp.dot(tile_sums, home_hot, precision=HIGH)
    volumes = lax.psum(partial_volumes, ("tx", "ty", "tz"))
    multiplier = grain_target - volumes / cells
    drive = jnp.dot(home_hot, multiplier, precision=HIGH)[:, None, None, None]
    for section_index in range(STEPS):
        face_xhigh = passed_along(
            remap(matched(neighbour_ids[0, 1, 1] - 1, plus_ids), phase[:, 0]), "tx", -1
        )
        face_xlow = passed_along(
            remap(matched(neighbour_ids[2, 1, 1] - 1, plus_ids), phase[:, -1]), "tx", 1
        )
        face_yhigh = passed_along(
            remap(matched(neighbour_ids[1, 0, 1] - 1, plus_ids), phase[:, :, 0]), "ty", -1
        )
        face_ylow = passed_along(
            remap(matched(neighbour_ids[1, 2, 1] - 1, plus_ids), phase[:, :, -1]), "ty", 1
        )
        face_zhigh = passed_along(
            remap(matched(neighbour_ids[1, 1, 0] - 1, plus_ids), phase[:, :, :, 0]), "tz", -1
        )
        face_zlow = passed_along(
            remap(matched(neighbour_ids[1, 1, 2] - 1, plus_ids), phase[:, :, :, -1]), "tz", 1
        )
        beside_all = jnp.concatenate([face_xlow[:, None], phase[:, :-1]], axis=1)
        beside_all = beside_all + jnp.concatenate([phase[:, 1:], face_xhigh[:, None]], axis=1)
        beside_all = beside_all + jnp.concatenate([face_ylow[:, :, None], phase[:, :, :-1]], axis=2)
        beside_all = beside_all + jnp.concatenate([phase[:, :, 1:], face_yhigh[:, :, None]], axis=2)
        beside_all = beside_all + jnp.concatenate([face_zlow[..., None], phase[..., :-1]], axis=3)
        beside_all = beside_all + jnp.concatenate([phase[..., 1:], face_zhigh[..., None]], axis=3)
        laplace = beside_all - 6.0 * phase
        weighted = weight_col * phase * phase
        pair = phase * weight_col * (jnp.sum(weighted, axis=0, keepdims=True) - weighted)
        update = phase + 0.1 * (laplace - 4.0 * pair + 2.0 * drive * phase * (1.0 - phase))
        update = jnp.maximum(update, 0.0)
        total = jnp.sum(update, axis=0, keepdims=True)
        phase = update / jnp.maximum(total, 1.0)
    return phase


def solution(mesh):
    return jax.shard_map(
        on_device,
        mesh=mesh,
        in_specs=(
            P(None, ("groups", "tx"), "ty", "tz"),
            P(("groups", "tx"), "ty", "tz", None),
            P(("groups", "tx"), "ty", "tz"),
            P("groups"),
            P("groups"),
            P("groups"),
        ),
        out_specs=P(None, ("groups", "tx"), "ty", "tz"),
        check_vma=False,
    )
```

profile of v0, /device:TPU:0, one launch (start us, length us, event | category | flops | bytes accessed | tf_op | source)
XLA Modules:
  0.0 137.2 jit_solution(6059207271199170311)
XLA Ops:
  0.7 0.7 fusion.96
  1.3 4.9 %collective-permute-start.2 = (s32[1,1,1,8]{3,2,1,0:T(1,128)S(1)}, s32[1,1,1,8]{3,2,1,0:T(1,128)S(1)}, u32[]{:S(2)}, u32[]{:S(2)}) collective-permute-start(s32[1,1,1,8]{3,2,1,0:T(1,128)S(1)} %fusion.96), channel_id=1, source_target_pairs={{0,4},{4,8},{8,12},{1,5},{5,9},{9,13},{2,6},{6,10},{10,14},{3,7},{... | collective-permute-start | bytes 104 | tf_op jit(solution)/shard_map/ppermute | solution.py:17
  6.3 1.3 collective-permute-start
  7.6 2.9 %fusion.108 = (f32[8]{0:T(128)S(1)}, f32[8,8,64,128]{3,0,2,1:T(8,128)S(1)}) fusion(f32[8]{0:T(128)S(1)} %fusion.99, f32[8,8,64,128]{3,2,1,0:T(8,128)} %param.6), kind=kLoop, calls=%fused_computation.155 | loop fusion | flops 1048568 | bytes 4194368 | tf_op jit(solution)/shard_map/reduce_sum | solution.py:57
  10.5 2.3 %fusion.113 = (f32[8,7,64,128]{3,0,2,1:T(8,128)}, f32[8,7,64,128]{3,0,2,1:T(8,128)}) fusion(f32[8,8,64,128]{3,0,2,1:T(8,128)S(1)} %get-tuple-element.10), kind=kLoop, calls=%fused_computation.160 | loop fusion | bytes 7340032 | tf_op jit(solution)/shard_map/slice | solution.py:81
  12.9 2.3 %fusion.114 = (f32[8,8,63,128]{3,0,2,1:T(8,128)}, f32[8,8,63,128]{3,0,2,1:T(8,128)}) fusion(f32[8,8,64,128]{3,0,2,1:T(8,128)S(1)} %get-tuple-element.10), kind=kLoop, calls=%fused_computation.161 | loop fusion | bytes 8257536 | tf_op jit(solution)/shard_map/slice | solution.py:83
  15.1 2.7 %fusion.115 = (f32[8,8,64,1]{3,0,2,1:T(8,128)}, f32[8,8,64,1]{3,0,2,1:T(8,128)}) fusion(f32[8,8,64,128]{3,0,2,1:T(8,128)S(1)} %get-tuple-element.10), kind=kLoop, calls=%fused_computation.162 | loop fusion | bytes 65536 | tf_op jit(solution)/shard_map/slice | solution.py:79
  17.8 2.6 %fusion.116 = (f32[8,8,64,127]{3,0,2,1:T(8,128)}, f32[8,8,64,127]{3,0,2,1:T(8,128)}) fusion(f32[8,8,64,128]{3,0,2,1:T(8,128)S(1)} %get-tuple-element.10), kind=kLoop, calls=%fused_computation.163 | loop fusion | bytes 8323072 | tf_op jit(solution)/shard_map/slice | solution.py:85
  20.5 0.2 select_reduce_fusion
  20.7 0.2 convolution_bitcast_fusion.1
  20.9 33.9 %psum.7 = f32[64]{0:T(128)S(1)} all-reduce(f32[64]{0:T(128)S(1)} %convolution_bitcast_fusion.1), channel_id=1, replica_groups=mesh['groups'=2,'tx'=4,'ty'=2,'tz'=2] {'tx','ty','tz'}, use_global_device_ids=true, to_apply=%region_3.4 | all-reduce | flops 64 | bytes 512 | tf_op jit(solution)/shard_map/psum | solution.py:59
  54.8 2.3 %copy.53 = f32[8,8,64,1]{2,0,1,3:T(8,128)S(1)} copy(f32[8,8,64,1]{3,0,2,1:T(8,128)} %get-tuple-element.25) | data formatting | bytes 32768 | tf_op jit(solution)/shard_map/squeeze | solution.py:79
  57.1 2.3 %copy.56 = f32[8,8,64,1]{2,0,1,3:T(8,128)S(1)} copy(f32[8,8,64,1]{3,0,2,1:T(8,128)} %get-tuple-element.26) | data formatting | bytes 32768 | tf_op jit(solution)/shard_map/squeeze | solution.py:76
  59.4 0.2 fusion.26
  59.6 0.0 collective-permute-done.2
  59.6 0.0 collective-permute-done
  59.6 1.3 collective-permute-start.6
  60.9 1.3 collective-permute-start.4
  62.2 0.3 fusion.32
  62.5 1.3 collective-permute-start.1
  63.9 0.3 fusion.31
  64.2 1.3 collective-permute-start.3
  65.5 0.9 collective-permute-done.4
  66.4 1.3 collective-permute-start.10
  67.7 1.3 collective-permute-start.8
  69.0 0.2 fusion.36
  69.2 3.7 %collective-permute-start.5 = (f32[8,8,128]{2,0,1:T(8,128)S(1)}, f32[8,8,128]{2,0,1:T(8,128)S(1)}, u32[]{:S(2)}, u32[]{:S(2)}) collective-permute-start(f32[8,8,128]{2,0,1:T(8,128)S(1)} %fusion.36), channel_id=1, source_target_pairs={{0,2},{1,3},{4,6},{5,7},{8,10},{9,11},{12,14},{13,15},{16,18},{17,... | collective-permute-start | bytes 98312 | tf_op jit(solution)/shard_map/ppermute | solution.py:28
  72.9 0.2 fusion.35
  73.1 0.0 collective-permute-done.8
  73.1 1.3 collective-permute-start.7
  74.5 0.2 fusion.43
  74.7 2.7 %collective-permute-start.9 = (f32[8,8,64]{2,0,1:T(8,128)S(1)}, f32[8,8,64]{2,0,1:T(8,128)S(1)}, u32[]{:S(2)}, u32[]{:S(2)}) collective-permute-start(f32[8,8,64]{2,0,1:T(8,128)S(1)} %fusion.43), channel_id=1, source_target_pairs={{0,1},{2,3},{4,5},{6,7},{8,9},{10,11},{12,13},{14,15},{16,17},{18,... | collective-permute-start | bytes 49160 | tf_op jit(solution)/shard_map/ppermute | solution.py:28
  77.4 0.2 fusion.41
  77.6 0.6 collective-permute-done.9
  78.3 1.3 collective-permute-start.11
  79.6 0.2 convolution_bitcast_fusion.2
  79.7 2.0 %copy.39 = f32[8,8,64,1]{3,0,2,1:T(8,128)} copy(f32[8,8,64,1]{2,0,1,3:T(8,128)S(1)} %bitcast.128) | data formatting | bytes 32768 | tf_op jit(solution)/shard_map/broadcast_in_dim | solution.py:85
  81.8 2.0 %copy.43 = f32[8,8,64,1]{3,0,2,1:T(8,128)} copy(f32[8,8,64,1]{2,0,1,3:T(8,128)S(1)} %bitcast.130) | data formatting | bytes 32768 | tf_op jit(solution)/shard_map/broadcast_in_dim | solution.py:86
  83.8 7.5 %fusion.106 = (f32[8,64,128]{2,1,0:T(8,128)S(1)}, f32[8,8,64,128]{3,0,2,1:T(8,128)S(1)}) fusion(f32[8,8,64,128]{3,0,2,1:T(8,128)S(1)} %get-tuple-element.10, f32[8]{0:T(128)S(1)} %fusion.26, f32[8]{0:T(128)S(1)} %convolution_bitcast_fusion.2, f32[8,8,64,1]{3,0,2,1:T(8,128)} %copy.43, f32[8,8,64,127]{3,0,2,1:T(8,128)} %get-tuple-element.28, ...), kind=kOutput, calls=%fused_computation.154 | output fusion | flops 15204359 | bytes 17039424 | tf_op jit(solution)/shard_map/sub | solution.py:89
  91.3 0.3 broadcast_divide_fusion.1
  91.7 0.2 fusion.33
  91.9 0.2 fusion.34
  92.1 0.3 fusion.29
  92.4 0.3 fusion.30
  92.7 2.3 %fusion.110 = (f32[8,8,63,128]{3,0,2,1:T(8,128)}, f32[8,8,63,128]{3,0,2,1:T(8,128)}) fusion(f32[8,8,64,128]{3,0,2,1:T(8,128)S(1)} %broadcast_divide_fusion.1), kind=kLoop, calls=%fused_computation.157 | loop fusion | bytes 8257536 | tf_op jit(solution)/shard_map/slice | solution.py:83
  95.0 2.7 %fusion.111 = (f32[8,8,64,1]{3,0,2,1:T(8,128)}, f32[8,8,64,1]{3,0,2,1:T(8,128)}) fusion(f32[8,8,64,128]{3,0,2,1:T(8,128)S(1)} %broadcast_divide_fusion.1), kind=kLoop, calls=%fused_computation.158 | loop fusion | bytes 65536 | tf_op jit(solution)/shard_map/slice | solution.py:79
  97.7 2.6 %fusion.112 = (f32[8,8,64,127]{3,0,2,1:T(8,128)}, f32[8,8,64,127]{3,0,2,1:T(8,128)}) fusion(f32[8,8,64,128]{3,0,2,1:T(8,128)S(1)} %broadcast_divide_fusion.1), kind=kLoop, calls=%fused_computation.159 | loop fusion | bytes 8323072 | tf_op jit(solution)/shard_map/slice | solution.py:85
  100.3 4.3 %collective-permute-start.14 = (f32[8,8,128]{2,0,1:T(8,128)S(1)}, f32[8,8,128]{2,0,1:T(8,128)S(1)}, u32[]{:S(2)}, u32[]{:S(2)}) collective-permute-start(f32[8,8,128]{2,0,1:T(8,128)S(1)} %fusion.34), channel_id=1, source_target_pairs={{0,2},{1,3},{4,6},{5,7},{8,10},{9,11},{12,14},{13,15},{16,18},{17,... | collective-permute-start | bytes 98312 | tf_op jit(solution)/shard_map/ppermute | solution.py:28
  104.6 1.3 collective-permute-start.15
  105.9 4.6 %collective-permute-start.12 = (f32[8,64,128]{2,0,1:T(8,128)S(1)}, f32[8,64,128]{2,0,1:T(8,128)S(1)}, u32[]{:S(2)}, u32[]{:S(2)}) collective-permute-start(f32[8,64,128]{2,0,1:T(8,128)S(1)} %fusion.30), channel_id=1, source_target_pairs={{0,4},{4,8},{8,12},{1,5},{5,9},{9,13},{2,6},{6,10},{10,14},{3,7},{... | collective-permute-start | bytes 786440 | tf_op jit(solution)/shard_map/ppermute | solution.py:28
  110.4 1.5 %collective-permute-start.13 = (f32[8,64,128]{2,0,1:T(8,128)S(1)}, f32[8,64,128]{2,0,1:T(8,128)S(1)}, u32[]{:S(2)}, u32[]{:S(2)}) collective-permute-start(f32[8,64,128]{2,0,1:T(8,128)S(1)} %fusion.29), channel_id=1, source_target_pairs={{4,0},{8,4},{12,8},{5,1},{9,5},{13,9},{6,2},{10,6},{14,10},{7,3},{... | collective-permute-start | bytes 786440 | tf_op jit(solution)/shard_map/ppermute | solution.py:28
  111.9 2.3 %copy.59 = f32[8,8,64,1]{2,0,1,3:T(8,128)S(1)} copy(f32[8,8,64,1]{3,0,2,1:T(8,128)} %get-tuple-element.17) | data formatting | bytes 32768 | tf_op jit(solution)/shard_map/squeeze | solution.py:79
  114.2 0.2 fusion.39
  114.4 2.3 %copy.62 = f32[8,8,64,1]{2,0,1,3:T(8,128)S(1)} copy(f32[8,8,64,1]{3,0,2,1:T(8,128)} %get-tuple-element.18) | data formatting | bytes 32768 | tf_op jit(solution)/shard_map/squeeze | solution.py:76
  116.7 2.5 %collective-permute-start.16 = (f32[8,8,64]{2,0,1:T(8,128)S(1)}, f32[8,8,64]{2,0,1:T(8,128)S(1)}, u32[]{:S(2)}, u32[]{:S(2)}) collective-permute-start(f32[8,8,64]{2,0,1:T(8,128)S(1)} %fusion.39), channel_id=1, source_target_pairs={{0,1},{2,3},{4,5},{6,7},{8,9},{10,11},{12,13},{14,15},{16,17},{18,... | collective-permute-start | bytes 49160 | tf_op jit(solution)/shard_map/ppermute | solution.py:28
  119.2 0.2 fusion.37
  119.4 0.6 collective-permute-done.16
  120.0 1.3 collective-permute-start.17
  121.3 2.3 %fusion.109 = (f32[8,7,64,128]{3,0,2,1:T(8,128)}, f32[8,7,64,128]{3,0,2,1:T(8,128)}) fusion(f32[8,8,64,128]{3,0,2,1:T(8,128)S(1)} %broadcast_divide_fusion.1), kind=kLoop, calls=%fused_computation.156 | loop fusion | bytes 7340032 | tf_op jit(solution)/shard_map/slice | solution.py:81
  123.6 2.0 %copy.47 = f32[8,8,64,1]{3,0,2,1:T(8,128)} copy(f32[8,8,64,1]{2,0,1,3:T(8,128)S(1)} %bitcast.127) | data formatting | bytes 32768 | tf_op jit(solution)/shard_map/broadcast_in_dim | solution.py:85
  125.7 2.0 %copy.51 = f32[8,8,64,1]{3,0,2,1:T(8,128)} copy(f32[8,8,64,1]{2,0,1,3:T(8,128)S(1)} %bitcast.129) | data formatting | bytes 32768 | tf_op jit(solution)/shard_map/broadcast_in_dim | solution.py:86
  127.7 7.5 %fusion.104 = (f32[8,64,128]{2,1,0:T(8,128)S(1)}, f32[8,8,64,128]{3,0,2,1:T(8,128)S(1)}) fusion(f32[8,8,64,128]{3,0,2,1:T(8,128)S(1)} %broadcast_divide_fusion.1, f32[8]{0:T(128)S(1)} %fusion.26, f32[8]{0:T(128)S(1)} %convolution_bitcast_fusion.2, f32[8,8,64,1]{3,0,2,1:T(8,128)} %copy.51, f32[8,8,64,127]{3,0,2,1:T(8,128)} %get-tuple-element.20, ...), kind=kOutput, calls=%fused_computation.153 | output fusion | flops 15204359 | bytes 17039424 | tf_op jit(solution)/shard_map/sub | solution.py:89
  135.2 0.3 broadcast_divide_fusion
  135.5 1.7 %copy.52 = f32[8,8,64,128]{3,2,1,0:T(8,128)} copy(f32[8,8,64,128]{3,0,2,1:T(8,128)S(1)} %broadcast_divide_fusion) | data formatting | bytes 4194304 | tf_op jit(solution)/shard_map/div | solution.py:93
  (37 shorter events, 0.2 us)
Async XLA Ops:
  0.0 79.6 %copy-start = (f32[64]{0:T(128)S(1)}, f32[64]{0:T(128)}, u32[]{:S(2)}) copy-start(f32[64]{0:T(128)} %param.10) | copy-start | bytes 772
  1.3 58.2 %collective-permute-start.2 = (s32[1,1,1,8]{3,2,1,0:T(1,128)S(1)}, s32[1,1,1,8]{3,2,1,0:T(1,128)S(1)}, u32[]{:S(2)}, u32[]{:S(2)}) collective-permute-start(s32[1,1,1,8]{3,2,1,0:T(1,128)S(1)} %fusion.96), channel_id=1, source_target_pairs={{0,4},{4,8},{8,12},{1,5},{5,9},{9,13},{2,6},{6,10},{10,14},{3,7},{... | collective-permute-start | bytes 104 | tf_op jit(solution)/shard_map/ppermute | solution.py:17
  6.3 53.3 %collective-permute-start = (s32[1,1,1,8]{3,2,1,0:T(1,128)S(1)}, s32[1,1,1,8]{3,2,1,0:T(1,128)S(1)}, u32[]{:S(2)}, u32[]{:S(2)}) collective-permute-start(s32[1,1,1,8]{3,2,1,0:T(1,128)S(1)} %fusion.96), channel_id=1, source_target_pairs={{4,0},{8,4},{12,8},{5,1},{9,5},{13,9},{6,2},{10,6},{14,10},{7,3},{... | collective-permute-start | bytes 104 | tf_op jit(solution)/shard_map/ppermute | solution.py:20
  17.8 2.6 %copy-start.1 = (s32[1,1,1,8]{3,2,1,0:T(1,128)S(1)}, s32[1,1,1,8]{3,2,1,0:T(1,128)}, u32[]{:S(2)}) copy-start(s32[1,1,1,8]{3,2,1,0:T(1,128)} %param.7) | copy-start | bytes 100
  17.8 2.6 %copy-start.2 = (s32[64]{0:T(128)S(1)}, s32[64]{0:T(128)}, u32[]{:S(2)}) copy-start(s32[64]{0:T(128)} %param.9) | copy-start | bytes 772
  54.8 4.6 %copy-start.3 = (f32[64]{0:T(128)S(1)}, f32[64]{0:T(128)}, u32[]{:S(2)}) copy-start(f32[64]{0:T(128)} %param.11) | copy-start | bytes 772
  59.6 5.9 %collective-permute-start.6 = (s32[3,1,1,8]{3,2,1,0:T(1,128)S(1)}, s32[3,1,1,8]{3,2,1,0:T(1,128)S(1)}, u32[]{:S(2)}, u32[]{:S(2)}) collective-permute-start(s32[3,1,1,8]{3,2,1,0:T(1,128)S(1)} %pad_add_fusion.1), channel_id=1, source_target_pairs={{0,2},{1,3},{4,6},{5,7},{8,10},{9,11},{12,14},{13,15},{16,18},{17,... | collective-permute-start | bytes 296 | tf_op jit(solution)/shard_map/ppermute | solution.py:17
  60.9 5.5 %collective-permute-start.4 = (s32[3,1,1,8]{3,2,1,0:T(1,128)S(1)}, s32[3,1,1,8]{3,2,1,0:T(1,128)S(1)}, u32[]{:S(2)}, u32[]{:S(2)}) collective-permute-start(s32[3,1,1,8]{3,2,1,0:T(1,128)S(1)} %pad_add_fusion.1), channel_id=1, source_target_pairs={{2,0},{3,1},{6,4},{7,5},{10,8},{11,9},{14,12},{15,13},{18,16},{19,... | collective-permute-start | bytes 296 | tf_op jit(solution)/shard_map/ppermute | solution.py:20
  62.5 21.3 %collective-permute-start.1 = (f32[8,64,128]{2,0,1:T(8,128)S(1)}, f32[8,64,128]{2,0,1:T(8,128)S(1)}, u32[]{:S(2)}, u32[]{:S(2)}) collective-permute-start(f32[8,64,128]{2,0,1:T(8,128)S(1)} %fusion.32), channel_id=1, source_target_pairs={{0,4},{4,8},{8,12},{1,5},{5,9},{9,13},{2,6},{6,10},{10,14},{3,7},{... | collective-permute-start | bytes 786440 | tf_op jit(solution)/shard_map/ppermute | solution.py:28
  64.2 19.6 %collective-permute-start.3 = (f32[8,64,128]{2,0,1:T(8,128)S(1)}, f32[8,64,128]{2,0,1:T(8,128)S(1)}, u32[]{:S(2)}, u32[]{:S(2)}) collective-permute-start(f32[8,64,128]{2,0,1:T(8,128)S(1)} %fusion.31), channel_id=1, source_target_pairs={{4,0},{8,4},{12,8},{5,1},{9,5},{13,9},{6,2},{10,6},{14,10},{7,3},{... | collective-permute-start | bytes 786440 | tf_op jit(solution)/shard_map/ppermute | solution.py:28
  66.4 8.3 %collective-permute-start.10 = (s32[3,3,1,8]{3,2,1,0:T(1,128)S(1)}, s32[3,3,1,8]{3,2,1,0:T(1,128)S(1)}, u32[]{:S(2)}, u32[]{:S(2)}) collective-permute-start(s32[3,3,1,8]{3,2,1,0:T(1,128)S(1)} %pad_add_fusion), channel_id=1, source_target_pairs={{0,1},{2,3},{4,5},{6,7},{8,9},{10,11},{12,13},{14,15},{16,17},{18,... | collective-permute-start | bytes 872 | tf_op jit(solution)/shard_map/ppermute | solution.py:17
  67.7 5.5 %collective-permute-start.8 = (s32[3,3,1,8]{3,2,1,0:T(1,128)S(1)}, s32[3,3,1,8]{3,2,1,0:T(1,128)S(1)}, u32[]{:S(2)}, u32[]{:S(2)}) collective-permute-start(s32[3,3,1,8]{3,2,1,0:T(1,128)S(1)} %pad_add_fusion), channel_id=1, source_target_pairs={{1,0},{3,2},{5,4},{7,6},{9,8},{11,10},{13,12},{15,14},{17,16},{19,... | collective-permute-start | bytes 872 | tf_op jit(solution)/shard_map/ppermute | solution.py:20
  69.2 14.6 %collective-permute-start.5 = (f32[8,8,128]{2,0,1:T(8,128)S(1)}, f32[8,8,128]{2,0,1:T(8,128)S(1)}, u32[]{:S(2)}, u32[]{:S(2)}) collective-permute-start(f32[8,8,128]{2,0,1:T(8,128)S(1)} %fusion.36), channel_id=1, source_target_pairs={{0,2},{1,3},{4,6},{5,7},{8,10},{9,11},{12,14},{13,15},{16,18},{17,... | collective-permute-start | bytes 98312 | tf_op jit(solution)/shard_map/ppermute | solution.py:28
  73.1 10.7 %collective-permute-start.7 = (f32[8,8,128]{2,0,1:T(8,128)S(1)}, f32[8,8,128]{2,0,1:T(8,128)S(1)}, u32[]{:S(2)}, u32[]{:S(2)}) collective-permute-start(f32[8,8,128]{2,0,1:T(8,128)S(1)} %fusion.35), channel_id=1, source_target_pairs={{2,0},{3,1},{6,4},{7,5},{10,8},{11,9},{14,12},{15,13},{18,16},{19,... | collective-permute-start | bytes 98312 | tf_op jit(solution)/shard_map/ppermute | solution.py:28
  74.7 3.6 %collective-permute-start.9 = (f32[8,8,64]{2,0,1:T(8,128)S(1)}, f32[8,8,64]{2,0,1:T(8,128)S(1)}, u32[]{:S(2)}, u32[]{:S(2)}) collective-permute-start(f32[8,8,64]{2,0,1:T(8,128)S(1)} %fusion.43), channel_id=1, source_target_pairs={{0,1},{2,3},{4,5},{6,7},{8,9},{10,11},{12,13},{14,15},{16,17},{18,... | collective-permute-start | bytes 49160 | tf_op jit(solution)/shard_map/ppermute | solution.py:28
  78.3 3.5 %collective-permute-start.11 = (f32[8,8,64]{2,0,1:T(8,128)S(1)}, f32[8,8,64]{2,0,1:T(8,128)S(1)}, u32[]{:S(2)}, u32[]{:S(2)}) collective-permute-start(f32[8,8,64]{2,0,1:T(8,128)S(1)} %fusion.41), channel_id=1, source_target_pairs={{1,0},{3,2},{5,4},{7,6},{9,8},{11,10},{13,12},{15,14},{17,16},{19,... | collective-permute-start | bytes 49160 | tf_op jit(solution)/shard_map/ppermute | solution.py:28
  100.3 27.4 %collective-permute-start.14 = (f32[8,8,128]{2,0,1:T(8,128)S(1)}, f32[8,8,128]{2,0,1:T(8,128)S(1)}, u32[]{:S(2)}, u32[]{:S(2)}) collective-permute-start(f32[8,8,128]{2,0,1:T(8,128)S(1)} %fusion.34), channel_id=1, source_target_pairs={{0,2},{1,3},{4,6},{5,7},{8,10},{9,11},{12,14},{13,15},{16,18},{17,... | collective-permute-start | bytes 98312 | tf_op jit(solution)/shard_map/ppermute | solution.py:28
  104.6 23.1 %collective-permute-start.15 = (f32[8,8,128]{2,0,1:T(8,128)S(1)}, f32[8,8,128]{2,0,1:T(8,128)S(1)}, u32[]{:S(2)}, u32[]{:S(2)}) collective-permute-start(f32[8,8,128]{2,0,1:T(8,128)S(1)} %fusion.33), channel_id=1, source_target_pairs={{2,0},{3,1},{6,4},{7,5},{10,8},{11,9},{14,12},{15,13},{18,16},{19,... | collective-permute-start | bytes 98312 | tf_op jit(solution)/shard_map/ppermute | solution.py:28
  105.9 21.8 %collective-permute-start.12 = (f32[8,64,128]{2,0,1:T(8,128)S(1)}, f32[8,64,128]{2,0,1:T(8,128)S(1)}, u32[]{:S(2)}, u32[]{:S(2)}) collective-permute-start(f32[8,64,128]{2,0,1:T(8,128)S(1)} %fusion.30), channel_id=1, source_target_pairs={{0,4},{4,8},{8,12},{1,5},{5,9},{9,13},{2,6},{6,10},{10,14},{3,7},{... | collective-permute-start | bytes 786440 | tf_op jit(solution)/shard_map/ppermute | solution.py:28
  110.4 17.3 %collective-permute-start.13 = (f32[8,64,128]{2,0,1:T(8,128)S(1)}, f32[8,64,128]{2,0,1:T(8,128)S(1)}, u32[]{:S(2)}, u32[]{:S(2)}) collective-permute-start(f32[8,64,128]{2,0,1:T(8,128)S(1)} %fusion.29), channel_id=1, source_target_pairs={{4,0},{8,4},{12,8},{5,1},{9,5},{13,9},{6,2},{10,6},{14,10},{7,3},{... | collective-permute-start | bytes 786440 | tf_op jit(solution)/shard_map/ppermute | solution.py:28
  116.7 3.3 %collective-permute-start.16 = (f32[8,8,64]{2,0,1:T(8,128)S(1)}, f32[8,8,64]{2,0,1:T(8,128)S(1)}, u32[]{:S(2)}, u32[]{:S(2)}) collective-permute-start(f32[8,8,64]{2,0,1:T(8,128)S(1)} %fusion.39), channel_id=1, source_target_pairs={{0,1},{2,3},{4,5},{6,7},{8,9},{10,11},{12,13},{14,15},{16,17},{18,... | collective-permute-start | bytes 49160 | tf_op jit(solution)/shard_map/ppermute | solution.py:28
  120.0 5.7 %collective-permute-start.17 = (f32[8,8,64]{2,0,1:T(8,128)S(1)}, f32[8,8,64]{2,0,1:T(8,128)S(1)}, u32[]{:S(2)}, u32[]{:S(2)}) collective-permute-start(f32[8,8,64]{2,0,1:T(8,128)S(1)} %fusion.37), channel_id=1, source_target_pairs={{1,0},{3,2},{5,4},{7,6},{9,8},{11,10},{13,12},{15,14},{17,16},{19,... | collective-permute-start | bytes 49160 | tf_op jit(solution)/shard_map/ppermute | solution.py:28
where the time goes:
time: 139 us; the launch traced here: 137 us
  local copies, waits for them, and re-layouts  38.8 us (28%)
  starting transfers between devices  38.3 us (28%)
  blocking collectives  33.9 us (24%)
  other arithmetic  19.5 us (14%)
  matrix products  3.46 us (2%)
  waiting for transfers between devices  2.17 us (2%)
    psum x1, blocking collectives, on_device(): volumes = lax.psum(partial_volumes, ('tx', 'ty', 'tz'))  33.9 us
    ppermute x12, starting transfers between devices, passed_along(): return lax.ppermute(block, axis, route)  26.9 us
    sub x2, other arithmetic, on_device(): jnp.sum(weighted, axis=0, keepdims=True) - weighted  14.9 us
    ppermute x3, starting transfers between devices, with_halo(): lax.ppermute(lax.slice_in_dim(block, block.shape[dim] - width, None, axis...  7.48 us
    slice x2, local copies, waits for them, and re-layouts, on_device(): phase[:, :, :, -1]  5.39 us
    slice x2, local copies, waits for them, and re-layouts, on_device(): phase[..., :-1]  5.25 us
    slice x2, local copies, waits for them, and re-layouts, on_device(): beside_all = jnp.concatenate([face_xlow[:, None], phase[:, :-1]], axis=1)  4.69 us
    squeeze x2, local copies, waits for them, and re-layouts, on_device(): phase[:, :, :, 0]  4.58 us
  transfers between devices with their start and end apart: 18, of which 3 were waited for; matrix products, arithmetic and copies ran while one was open for 26% of the time, Pallas kernels for 0%

commit v1 on v0

v1 whole, which is shorter than its diff:
```python
import functools

import jax
import jax.numpy as jnp
from jax import lax
from jax.experimental import pallas as pl
from jax.experimental.pallas import tpu as pltpu
from jax.sharding import PartitionSpec as P

MESH = pl.DeviceIdType.MESH
CHUNKS = 4
PAD = 8


def each(low, high, body):
    if high - low <= 32:
        for k in range(low, high):
            body(k)
    else:
        pl.loop(low, high)(body)


def kernel(
    sizes, phase, grain, crowd, home, weight, target, out,
    first, second, msg, places, place, coef, xin, yin, zin, zout,
    load_sem, msg_send, msg_recv, place_sem, x_send, x_recv, y_send, y_recv,
    z_send, z_recv, out_sem,
):
    tiles_x, tiles_y, tiles_z = sizes
    slots, cx, cy, cz = phase.shape
    cells = cx * cy * cz
    tiles = tiles_x * tiles_y * tiles_z
    rows = cy // CHUNKS
    tx, ty, tz = (lax.axis_index(a) for a in ("tx", "ty", "tz"))
    me = (tx * tiles_y + ty) * tiles_z + tz
    inner = pl.ds(PAD, cy)

    def partner(k):
        other = lax.rem(me + k, tiles)
        return {
            "tx": lax.div(other, tiles_y * tiles_z),
            "ty": lax.rem(lax.div(other, tiles_z), tiles_y),
            "tz": lax.rem(other, tiles_z),
        }

    loads = [
        pltpu.make_async_copy(phase.at[s], first.at[s, pl.ds(1, cx), inner], load_sem.at[s])
        for s in range(slots)
    ]
    for load in loads:
        load.start()

    barrier = pltpu.get_barrier_semaphore()

    def greet(k):
        pl.semaphore_signal(barrier, inc=1, device_id=partner(k), device_id_type=MESH)

    each(1, tiles, greet)

    for buffer in xin:
        buffer[slots] = jnp.zeros(buffer.shape[1:], jnp.float32)
    for buffer in yin:
        buffer[slots] = jnp.zeros(buffer.shape[1:], jnp.float32)
    for buffer in zin:
        buffer[slots] = jnp.zeros(buffer.shape[1:], jnp.float32)
    live_count = crowd[0, 0, 0]
    row = lax.broadcasted_iota(jnp.int32, (8, cz), 0)
    lane = lax.broadcasted_iota(jnp.int32, (8, cz), 1)
    live = [s < live_count for s in range(slots)]
    ids = [jnp.where(live[s], grain[0, 0, 0, s], -1).astype(jnp.float32) for s in range(slots)]
    mine = [jnp.where(live[s], ids[s], -2.0) for s in range(slots)]
    id_rows = jnp.full((8, cz), -1.0, jnp.float32)
    mine_lanes = jnp.full((8, cz), -2.0, jnp.float32)
    for s in range(slots):
        id_rows = jnp.where(row == s, ids[s], id_rows)
        mine_lanes = jnp.where(lane == s, mine[s], mine_lanes)
    msg[0, 1] = id_rows

    pl.semaphore_wait(barrier, tiles - 1)

    goes = ((tx < tiles_x - 1, ty < tiles_y - 1), (tx > 0, ty > 0))
    comes = ((tx > 0, ty > 0), (tx < tiles_x - 1, ty < tiles_y - 1))
    to = (({"tx": tx + 1}, {"ty": ty + 1}), ({"tx": tx - 1}, {"ty": ty - 1}))

    def x_copy(step, side, c):
        start = c * rows
        if step == 0:
            src = phase.at[:, (cx - 1, 0)[side], pl.ds(start, rows)]
        else:
            src = second.at[:, (cx, 1)[side], pl.ds(PAD + start, rows)]
        at = (step * 2 + side) * CHUNKS + c
        return pltpu.make_async_remote_copy(
            src, xin[at].at[pl.ds(0, slots)], x_send.at[at], x_recv.at[at],
            device_id=to[side][0], device_id_type=MESH,
        )

    def y_copy(step, side):
        at_row = (cy - 1, 0)[side]
        if step == 0:
            src = phase.at[:, :, pl.ds(at_row, 1)]
        else:
            src = second.at[:, pl.ds(1, cx), pl.ds(PAD + at_row, 1)]
        at = step * 2 + side
        return pltpu.make_async_remote_copy(
            src, yin[at].at[pl.ds(0, slots), :, pl.ds(0, 1)], y_send.at[at], y_recv.at[at],
            device_id=to[side][1], device_id_type=MESH,
        )

    def z_copy(step):
        return pltpu.make_async_remote_copy(
            zout[step], zin[step].at[pl.ds(0, slots)], z_send.at[step], z_recv.at[step],
            device_id={"tz": 1 - tz}, device_id_type=MESH,
        )

    def send_x(step, c):
        for side in range(2):
            pl.when(goes[side][0])(lambda: x_copy(step, side, c).start())

    def send_y(step):
        for side in range(2):
            pl.when(goes[side][1])(lambda: y_copy(step, side).start())

    send_y(0)
    send_x(0, 0)

    face_lane = jnp.where(tz == 0, cz - 1, 0)
    lane3 = lax.broadcasted_iota(jnp.int32, (cy, cz), 1)
    z_face = lane3 == face_lane

    def z_part(value, x):
        part = jnp.where(z_face, value, 0.0)
        total = jnp.zeros((8, cz), jnp.float32)
        for t in range(cy // 8):
            total = total + pltpu.roll(part[t * 8:t * 8 + 8], 2 * (x + cx * t), 1)
        return total

    for s in range(slots):
        loads[s].wait()
        factor = jnp.where(live[s], 1.0, 0.0).astype(jnp.float32)

        def clear(x, carry):
            total, face = carry
            value = first[s, x + 1, inner] * factor
            first[s, x + 1, inner] = value
            total = total + jnp.sum(value.reshape(cy // 8, 8, cz), axis=0)
            return total, face + z_part(value, x)

        zero = jnp.zeros((8, cz), jnp.float32)
        total, face = lax.fori_loop(0, cx, clear, (zero, zero))
        zout[0][s] = face
        msg[0, 0, s:s + 1] = jnp.sum(total, axis=0, keepdims=True)

    def msg_copy(k):
        return pltpu.make_async_remote_copy(
            msg.at[0], msg.at[k], msg_send.at[k], msg_recv.at[k],
            device_id=partner(k), device_id_type=MESH,
        )

    each(1, tiles, lambda k: msg_copy(k).start())
    z_copy(0).start()
    for c in range(1, CHUNKS):
        send_x(0, c)
    each(1, tiles, lambda k: msg_copy(k).wait_recv())

    plane = tiles_y * tiles_z
    froms = (
        (plane, comes[0][0]), (tiles - plane, comes[1][0]),
        (tiles_z, comes[0][1]), (tiles - tiles_z, comes[1][1]),
        (tiles - 1, tz == 0), (1, tz == 1),
    )
    table = jnp.zeros((8, cz), jnp.int32)
    for f, (k, there) in enumerate(froms):
        same = (msg[k % tiles, 1] == mine_lanes) & there
        found = jnp.max(jnp.where(same, slots - row, 0), axis=0, keepdims=True)
        table = jnp.where(row == f, slots - found, table)
    places[...] = table
    to_scalars = pltpu.make_async_copy(places, place, place_sem)
    to_scalars.start()

    def add_tile(k, sums):
        ids_k, sums_k = msg[k, 1], msg[k, 0]
        return tuple(
            sums[s] + jnp.where(ids_k == mine[s], sums_k, 0.0) for s in range(slots)
        )

    sums = lax.fori_loop(
        0, tiles, add_tile, (jnp.zeros((8, cz), jnp.float32),) * slots,
        unroll=4 if tiles % 4 == 0 else 1,
    )
    for s in range(slots):
        g = grain[0, 0, 0, s]
        volume = jnp.sum(jnp.sum(sums[s], axis=0, keepdims=True), axis=1, keepdims=True)
        drive = jnp.where(live[s], target[home[g]] - volume * (1.0 / cells), 0.0)
        w = jnp.where(live[s], weight[g], 0.0)
        coef[0, s] = jnp.broadcast_to(0.4 + 0.2 * drive, (8, cz))
        coef[1, s] = jnp.broadcast_to(0.2 * drive, (8, cz))
        coef[2, s] = jnp.full((8, cz), w, jnp.float32)
        coef[3, s] = jnp.full((8, cz), 0.4 * w, jnp.float32)
    to_scalars.wait()

    lane_chunk = lax.broadcasted_iota(jnp.int32, (rows, cz), 1)
    low_lane, high_lane = lane_chunk == 0, lane_chunk == cz - 1

    def advance(step, src, dst, c, x):
        start = PAD + c * rows
        faces = zin[step]
        sub = rows // 8
        wide = lambda i, s: jnp.concatenate([coef[i, s]] * sub, axis=0)
        held, squares, mixed = [], [], jnp.zeros((rows, cz), jnp.float32)
        for s in range(slots):
            p = src[s, x, pl.ds(start, rows)]
            square = wide(2, s) * (p * p)
            mixed = mixed + square
            held.append(p)
            squares.append(square)
        total = jnp.zeros((rows, cz), jnp.float32)
        updates = []
        for s in range(slots):
            p = held[s]
            face = faces[jnp.where(tz == 0, place[4, s], place[5, s])]
            ghost = jnp.concatenate([
                pltpu.roll(face, lax.rem(2 * cz - 2 * ((x - 1) + cx * (c * sub + t)), cz), 1)
                for t in range(sub)
            ], axis=0)
            beside = pltpu.roll(jnp.where(low_lane, ghost, p), cz - 1, 1)
            beside = beside + pltpu.roll(jnp.where(high_lane, ghost, p), 1, 1)
            beside = beside + src[s, x, pl.ds(start - 1, rows)]
            beside = beside + src[s, x, pl.ds(start + 1, rows)]
            beside = beside + src[s, x - 1, pl.ds(start, rows)]
            beside = beside + src[s, x + 1, pl.ds(start, rows)]
            slope = wide(0, s) - wide(1, s) * p - wide(3, s) * (mixed - squares[s])
            update = jnp.maximum(0.1 * beside + p * slope, 0.0)
            total = total + update
            updates.append(update)
        scale = 1.0 / jnp.maximum(total, 1.0)
        for s in range(slots):
            dst[s, x, pl.ds(start, rows)] = updates[s] * scale

    def take_yz(step, src):
        z_copy(step).wait_recv()
        for side in range(2):
            pl.when(comes[side][1])(lambda: y_copy(step, side).wait_recv())
        for side in range(2):
            for s in range(slots):
                ghost_row = (PAD - 1, PAD + cy)[side]
                src[s, pl.ds(1, cx), pl.ds(ghost_row, 1)] = yin[step * 2 + side][
                    place[2 + side, s], :, pl.ds(0, 1)
                ]

    def take_x(step, src, c):
        for side in range(2):
            pl.when(comes[side][0])(lambda: x_copy(step, side, c).wait_recv())
            for s in range(slots):
                src[s, (0, cx + 1)[side], pl.ds(PAD + c * rows, rows)] = xin[
                    (step * 2 + side) * CHUNKS + c
                ][place[side, s]]

    take_yz(0, first)
    for c in range(CHUNKS):
        take_x(0, first, c)
        pl.loop(0, 2)(lambda i: advance(0, first, second, c, 1 + i * (cx - 1)))
        send_x(1, c)
        pl.loop(2, cx)(lambda x: advance(0, first, second, c, x))
    send_y(1)
    for s in range(slots):
        zout[1][s] = lax.fori_loop(
            0, cx, lambda x, face: face + z_part(second[s, x + 1, inner], x),
            jnp.zeros((8, cz), jnp.float32),
        )
    z_copy(1).start()

    def out_copy(i, x, start, count):
        return pltpu.make_async_copy(
            first.at[:, x, pl.ds(PAD + start, count)],
            out.at[:, x - 1, pl.ds(start, count)], out_sem.at[i],
        )

    take_yz(1, second)
    outs = []
    for c in range(CHUNKS):
        pl.loop(2, cx)(lambda x: advance(1, second, first, c, x))
        copy = pltpu.make_async_copy(
            first.at[:, pl.ds(2, cx - 2), pl.ds(PAD + c * rows, rows)],
            out.at[:, pl.ds(1, cx - 2), pl.ds(c * rows, rows)], out_sem.at[c],
        )
        copy.start()
        outs.append(copy)
    for c in range(CHUNKS):
        take_x(1, second, c)
        pl.loop(0, 2)(lambda i: advance(1, second, first, c, 1 + i * (cx - 1)))
        for i, x in enumerate((1, cx)):
            copy = out_copy(CHUNKS * (1 + i) + c, x, c * rows, rows)
            copy.start()
            outs.append(copy)

    each(1, tiles, lambda k: msg_copy(k).wait_send())
    for step in range(2):
        z_copy(step).wait_send()
        for side in range(2):
            pl.when(goes[side][1])(lambda: y_copy(step, side).wait_send())
            for c in range(CHUNKS):
                pl.when(goes[side][0])(lambda: x_copy(step, side, c).wait_send())
    for copy in outs:
        copy.wait()


def on_device(sizes, phase, slot_grain, crowding, grain_home, grain_weight, grain_target):
    slots, cx, cy, cz = phase.shape
    tiles = sizes[0] * sizes[1] * sizes[2]
    field = pltpu.VMEM((slots, cx + 2, cy + 2 * PAD, cz), jnp.float32)
    dma = pltpu.SemaphoreType.DMA
    any_space = pl.BlockSpec(memory_space=pl.ANY)
    scalars = pl.BlockSpec(memory_space=pltpu.SMEM)
    return pl.pallas_call(
        functools.partial(kernel, sizes),
        out_shape=jax.ShapeDtypeStruct(phase.shape, jnp.float32),
        in_specs=[any_space] + [scalars] * 5,
        out_specs=any_space,
        scratch_shapes=[
            field, field,
            pltpu.VMEM((tiles, 2, 8, cz), jnp.float32),
            pltpu.VMEM((8, cz), jnp.int32),
            pltpu.SMEM((8, cz), jnp.int32),
            pltpu.VMEM((4, slots, 8, cz), jnp.float32),
            [pltpu.VMEM((slots + 1, cy // CHUNKS, cz), jnp.float32)] * (4 * CHUNKS),
            [pltpu.VMEM((slots + 1, cx, 8, cz), jnp.float32)] * 4,
            [pltpu.VMEM((slots + 1, 8, cz), jnp.float32)] * 2,
            [pltpu.VMEM((slots, 8, cz), jnp.float32)] * 2,
            dma((slots,)), dma((tiles,)), dma((tiles,)), dma,
            dma((4 * CHUNKS,)), dma((4 * CHUNKS,)), dma((4,)), dma((4,)),
            dma((2,)), dma((2,)), dma((3 * CHUNKS,)),
        ],
        compiler_params=pltpu.CompilerParams(
            collective_id=0, has_side_effects=True, vmem_limit_bytes=40 * 2**20
        ),
    )(phase, slot_grain, crowding, grain_home, grain_weight, grain_target)


def solution(mesh):
    sizes = tuple(mesh.shape[a] for a in ("tx", "ty", "tz"))
    return jax.shard_map(
        functools.partial(on_device, sizes),
        mesh=mesh,
        in_specs=(
            P(None, ("groups", "tx"), "ty", "tz"),
            P(("groups", "tx"), "ty", "tz", None),
            P(("groups", "tx"), "ty", "tz"),
            P("groups"),
            P("groups"),
            P("groups"),
        ),
        out_specs=P(None, ("groups", "tx"), "ty", "tz"),
        check_vma=False,
    )
```

time: 139 us -> 42.3 us (0.30); the launches traced: 137 us -> 42.2 us
  starting transfers between devices: 38.3 us -> 0 us
  Pallas kernels: 0 us -> 36 us
  blocking collectives: 33.9 us -> 0 us
  local copies, waits for them, and re-layouts: 38.8 us -> 5.52 us
  other arithmetic: 19.5 us -> 0 us
  matrix products: 3.46 us -> 0 us
  waiting for transfers between devices: 2.17 us -> 0 us
    ppermute x18 -> x0, starting transfers between devices: 38.3 us -> none  [the longest x12 26.9 us: passed_along(): return lax.ppermute(block, axis, route)]
    pallas_call x0 -> x1, Pallas kernels: none -> 36 us  [on_device(): pl.pallas_call(functools.partial(kernel, sizes), out_shape=jax.ShapeDtype...]
    psum x1 -> x0, blocking collectives: 33.9 us -> none  [on_device(): volumes = lax.psum(partial_volumes, ('tx', 'ty', 'tz'))]
    slice x8 -> x0, local copies, waits for them, and re-layouts: 19.9 us -> none  [the longest x2 5.39 us: on_device(): phase[:, :, :, -1]]
    sub x2 -> x0, other arithmetic: 14.9 us -> none  [on_device(): jnp.sum(weighted, axis=0, keepdims=True) - weighted]
    squeeze x8 -> x0, local copies, waits for them, and re-layouts: 9.16 us -> none  [the longest x2 4.58 us: on_device(): phase[:, :, :, 0]]
    broadcast_in_dim x4 -> x0, local copies, waits for them, and re-layouts: 8.1 us -> none  [the longest x2 4.07 us: on_device(): face_zlow[..., None]]
    unnamed x8 -> x11, local copies, waits for them, and re-layouts: 0.02 us -> 5.52 us
  transfers between devices with their start and end apart: 18 -> 0, of which waited for: 3 -> 0; matrix products, arithmetic and copies ran while one was open for 26% -> 0% of each run, Pallas kernels for 0% -> 0%
where the time goes in v1:
time: 42.3 us; the launch traced here: 42.2 us
  Pallas kernels  36 us (85%)
  local copies, waits for them, and re-layouts  5.52 us (13%)
  between operations  0.67 us (2%)
    pallas_call x1, Pallas kernels, on_device(): pl.pallas_call(functools.partial(kernel, sizes), out_shape=jax.ShapeDtype...  36 us
    unnamed x11, local copies, waits for them, and re-layouts  5.52 us

profile of v1, /device:TPU:0, one launch (start us, length us, event | category | flops | bytes accessed | tf_op | source)
XLA Modules:
  0.0 42.2 jit_solution(1125840843841411870)
XLA Ops:
  0.7 0.0 copy-start
  0.7 1.6 %copy-done = f32[8,8,64,128]{3,2,1,0:T(8,128)S(1)} copy-done((f32[8,8,64,128]{3,2,1,0:T(8,128)S(1)}, f32[8,8,64,128]{3,2,1,0:T(8,128)}, u32[]{:S(2)}) %copy-start) | copy-done | bytes 2097176
  2.2 0.0 copy-start.1
  2.2 0.7 %copy-done.1 = s32[1,1,1,8]{3,2,1,0:T(1,128)S(1)} copy-done((s32[1,1,1,8]{3,2,1,0:T(1,128)S(1)}, s32[1,1,1,8]{3,2,1,0:T(1,128)}, u32[]{:S(2)}) %copy-start.1) | copy-done | bytes 56
  2.9 0.0 copy-start.2
  2.9 0.7 %copy-done.2 = s32[64]{0:T(128)S(1)} copy-done((s32[64]{0:T(128)S(1)}, s32[64]{0:T(128)}, u32[]{:S(2)}) %copy-start.2) | copy-done | bytes 280
  3.6 0.0 copy-start.3
  3.6 0.7 %copy-done.3 = f32[64]{0:T(128)S(1)} copy-done((f32[64]{0:T(128)S(1)}, f32[64]{0:T(128)}, u32[]{:S(2)}) %copy-start.3) | copy-done | bytes 280
  4.2 0.0 copy-start.4
  4.2 0.7 %copy-done.4 = f32[64]{0:T(128)S(1)} copy-done((f32[64]{0:T(128)S(1)}, f32[64]{0:T(128)}, u32[]{:S(2)}) %copy-start.4) | copy-done | bytes 280
  4.9 36.0 %shard_map.64 = f32[8,8,64,128]{3,2,1,0:T(8,128)S(1)} custom-call(f32[8,8,64,128]{3,2,1,0:T(8,128)S(1)} %copy-done, s32[1,1,1,8]{3,2,1,0:T(1,128)S(1)} %copy-done.1, s32[1,1,1]{2,1,0:T(1,128)S(6)} %copy.8.crowd, s32[64]{0:T(128)S(1)} %copy-done.2, f32[64]{0:T(128)S(1)} %copy-done.3, f32[64]{0:T(128)S(1)} %copy-done.4), custom_call_target="tpu_custom_call" | custom-call | tf_op jit(solution)/shard_map/pallas_call | solution.py:314
  40.8 1.3 %copy.9 = f32[8,8,64,128]{3,2,1,0:T(8,128)} copy(f32[8,8,64,128]{3,2,1,0:T(8,128)S(1)} %shard_map.64) | data formatting | bytes 4194304
Async XLA Ops:
  0.7 1.6 %copy-start = (f32[8,8,64,128]{3,2,1,0:T(8,128)S(1)}, f32[8,8,64,128]{3,2,1,0:T(8,128)}, u32[]{:S(2)}) copy-start(f32[8,8,64,128]{3,2,1,0:T(8,128)} %phase.1) | copy-start | bytes 6291460
  2.2 0.7 %copy-start.1 = (s32[1,1,1,8]{3,2,1,0:T(1,128)S(1)}, s32[1,1,1,8]{3,2,1,0:T(1,128)}, u32[]{:S(2)}) copy-start(s32[1,1,1,8]{3,2,1,0:T(1,128)} %grain.1) | copy-start | bytes 100
  2.9 0.7 %copy-start.2 = (s32[64]{0:T(128)S(1)}, s32[64]{0:T(128)}, u32[]{:S(2)}) copy-start(s32[64]{0:T(128)} %home.1) | copy-start | bytes 772
  3.6 0.7 %copy-start.3 = (f32[64]{0:T(128)S(1)}, f32[64]{0:T(128)}, u32[]{:S(2)}) copy-start(f32[64]{0:T(128)} %weight.1) | copy-start | bytes 772
  4.2 0.7 %copy-start.4 = (f32[64]{0:T(128)S(1)}, f32[64]{0:T(128)}, u32[]{:S(2)}) copy-start(f32[64]{0:T(128)} %target.1) | copy-start | bytes 772

commit v2 on v1

--- a/solution.py
+++ b/solution.py
@@ -21,9 +21,9 @@
 
 
 def kernel(
-    sizes, phase, grain, crowd, home, weight, target, out,
-    first, second, msg, places, place, coef, xin, yin, zin, zout,
-    load_sem, msg_send, msg_recv, place_sem, x_send, x_recv, y_send, y_recv,
+    sizes, phase, grain_in, crowd_in, home_in, weight_in, target_in, out,
+    grain, crowd, home, weight, target, first, second, msg, places, place, coef, xin, yin, zin, zout,
+    small_sem, load_sem, msg_send, msg_recv, place_sem, x_send, x_recv, y_send, y_recv,
     z_send, z_recv, out_sem,
 ):
     tiles_x, tiles_y, tiles_z = sizes
@@ -43,6 +43,15 @@
             "tz": lax.rem(other, tiles_z),
         }
 
+    smalls = [
+        pltpu.make_async_copy(src, dst, small_sem.at[i])
+        for i, (src, dst) in enumerate((
+            (crowd_in, crowd), (grain_in, grain), (home_in, home),
+            (weight_in, weight), (target_in, target),
+        ))
+    ]
+    for small in smalls:
+        small.start()
     loads = [
         pltpu.make_async_copy(phase.at[s], first.at[s, pl.ds(1, cx), inner], load_sem.at[s])
         for s in range(slots)
@@ -63,6 +72,8 @@
         buffer[slots] = jnp.zeros(buffer.shape[1:], jnp.float32)
     for buffer in zin:
         buffer[slots] = jnp.zeros(buffer.shape[1:], jnp.float32)
+    for small in smalls:
+        small.wait()
     live_count = crowd[0, 0, 0]
     row = lax.broadcasted_iota(jnp.int32, (8, cz), 0)
     lane = lax.broadcasted_iota(jnp.int32, (8, cz), 1)
@@ -123,32 +134,13 @@
     send_y(0)
     send_x(0, 0)
 
-    face_lane = jnp.where(tz == 0, cz - 1, 0)
-    lane3 = lax.broadcasted_iota(jnp.int32, (cy, cz), 1)
-    z_face = lane3 == face_lane
-
-    def z_part(value, x):
-        part = jnp.where(z_face, value, 0.0)
-        total = jnp.zeros((8, cz), jnp.float32)
-        for t in range(cy // 8):
-            total = total + pltpu.roll(part[t * 8:t * 8 + 8], 2 * (x + cx * t), 1)
-        return total
-
     for s in range(slots):
         loads[s].wait()
-        factor = jnp.where(live[s], 1.0, 0.0).astype(jnp.float32)
-
-        def clear(x, carry):
-            total, face = carry
-            value = first[s, x + 1, inner] * factor
-            first[s, x + 1, inner] = value
-            total = total + jnp.sum(value.reshape(cy // 8, 8, cz), axis=0)
-            return total, face + z_part(value, x)
-
-        zero = jnp.zeros((8, cz), jnp.float32)
-        total, face = lax.fori_loop(0, cx, clear, (zero, zero))
-        zout[0][s] = face
-        msg[0, 0, s:s + 1] = jnp.sum(total, axis=0, keepdims=True)
+        parts = [jnp.sum(first[s, x + 1, inner].reshape(cy // 8, 8, cz), axis=0) for x in range(cx)]
+        while len(parts) > 1:
+            parts = [a + b for a, b in zip(parts[::2], parts[1::2])]
+        total = jnp.where(live[s], jnp.sum(parts[0], axis=0, keepdims=True), 0.0)
+        msg[0, 0, s:s + 1] = total
 
     def msg_copy(k):
         return pltpu.make_async_remote_copy(
@@ -157,7 +149,26 @@
         )
 
     each(1, tiles, lambda k: msg_copy(k).start())
-    z_copy(0).start()
+
+    z_face = lane == jnp.where(tz == 0, cz - 1, 0)
+
+    def pack_z(step, src):
+        @pl.loop(0, slots)
+        def _(s):
+            parts = []
+            for x in range(cx):
+                for t in range(cy // 8):
+                    value = src[s, x + 1, pl.ds(PAD + 8 * t, 8)]
+                    part = jnp.where(z_face, value, 0.0)
+                    k = x + cx * t
+                    parts.append(pltpu.roll(part, 2 * k, 1) if k else part)
+            while len(parts) > 1:
+                parts = [a + b for a, b in zip(parts[::2], parts[1::2])]
+            zout[step][s] = parts[0]
+
+        z_copy(step).start()
+
+    pack_z(0, first)
     for c in range(1, CHUNKS):
         send_x(0, c)
     each(1, tiles, lambda k: msg_copy(k).wait_recv())
@@ -192,49 +203,46 @@
         volume = jnp.sum(jnp.sum(sums[s], axis=0, keepdims=True), axis=1, keepdims=True)
         drive = jnp.where(live[s], target[home[g]] - volume * (1.0 / cells), 0.0)
         w = jnp.where(live[s], weight[g], 0.0)
-        coef[0, s] = jnp.broadcast_to(0.4 + 0.2 * drive, (8, cz))
+        coef[0, s] = jnp.broadcast_to(jnp.where(live[s], 0.4 + 0.2 * drive, 0.0), (8, cz))
         coef[1, s] = jnp.broadcast_to(0.2 * drive, (8, cz))
         coef[2, s] = jnp.full((8, cz), w, jnp.float32)
         coef[3, s] = jnp.full((8, cz), 0.4 * w, jnp.float32)
+        coef[4, s] = jnp.full((8, cz), jnp.where(live[s], 0.1, 0.0), jnp.float32)
     to_scalars.wait()
-
-    lane_chunk = lax.broadcasted_iota(jnp.int32, (rows, cz), 1)
-    low_lane, high_lane = lane_chunk == 0, lane_chunk == cz - 1
+    z_place = [jnp.where(tz == 0, place[4, s], place[5, s]) for s in range(slots)]
+
+    low_lane, high_lane = lane == 0, lane == cz - 1
 
     def advance(step, src, dst, c, x):
-        start = PAD + c * rows
+        for t in range(rows // 8):
+            advance_rows(step, src, dst, c * (rows // 8) + t, x)
+
+    def advance_rows(step, src, dst, t, x):
+        start = PAD + 8 * t
         faces = zin[step]
-        sub = rows // 8
-        wide = lambda i, s: jnp.concatenate([coef[i, s]] * sub, axis=0)
-        held, squares, mixed = [], [], jnp.zeros((rows, cz), jnp.float32)
+        turn = lax.rem(2 * cz - 2 * ((x - 1) + cx * t), cz)
+        squares, mixed = [], jnp.zeros((8, cz), jnp.float32)
         for s in range(slots):
-            p = src[s, x, pl.ds(start, rows)]
-            square = wide(2, s) * (p * p)
+            p = src[s, x, pl.ds(start, 8)]
+            square = coef[2, s] * (p * p)
             mixed = mixed + square
-            held.append(p)
             squares.append(square)
-        total = jnp.zeros((rows, cz), jnp.float32)
+        total = jnp.zeros((8, cz), jnp.float32)
         updates = []
         for s in range(slots):
-            p = held[s]
-            face = faces[jnp.where(tz == 0, place[4, s], place[5, s])]
-            ghost = jnp.concatenate([
-                pltpu.roll(face, lax.rem(2 * cz - 2 * ((x - 1) + cx * (c * sub + t)), cz), 1)
-                for t in range(sub)
-            ], axis=0)
+            p = src[s, x, pl.ds(start, 8)]
+            ghost = pltpu.roll(faces[z_place[s]], turn, 1)
             beside = pltpu.roll(jnp.where(low_lane, ghost, p), cz - 1, 1)
             beside = beside + pltpu.roll(jnp.where(high_lane, ghost, p), 1, 1)
-            beside = beside + src[s, x, pl.ds(start - 1, rows)]
-            beside = beside + src[s, x, pl.ds(start + 1, rows)]
-            beside = beside + src[s, x - 1, pl.ds(start, rows)]
-            beside = beside + src[s, x + 1, pl.ds(start, rows)]
-            slope = wide(0, s) - wide(1, s) * p - wide(3, s) * (mixed - squares[s])
-            update = jnp.maximum(0.1 * beside + p * slope, 0.0)
+            beside = beside + (src[s, x, pl.ds(start - 1, 8)] + src[s, x, pl.ds(start + 1, 8)])
+            beside = beside + (src[s, x - 1, pl.ds(start, 8)] + src[s, x + 1, pl.ds(start, 8)])
+            slope = coef[0, s] - coef[1, s] * p - coef[3, s] * (mixed - squares[s])
+            update = jnp.maximum(coef[4, s] * beside + p * slope, 0.0)
             total = total + update
             updates.append(update)
         scale = 1.0 / jnp.maximum(total, 1.0)
         for s in range(slots):
-            dst[s, x, pl.ds(start, rows)] = updates[s] * scale
+            dst[s, x, pl.ds(start, 8)] = updates[s] * scale
 
     def take_yz(step, src):
         z_copy(step).wait_recv()
@@ -262,12 +270,7 @@
         send_x(1, c)
         pl.loop(2, cx)(lambda x: advance(0, first, second, c, x))
     send_y(1)
-    for s in range(slots):
-        zout[1][s] = lax.fori_loop(
-            0, cx, lambda x, face: face + z_part(second[s, x + 1, inner], x),
-            jnp.zeros((8, cz), jnp.float32),
-        )
-    z_copy(1).start()
+    pack_z(1, second)
 
     def out_copy(i, x, start, count):
         return pltpu.make_async_copy(
@@ -310,28 +313,31 @@
     field = pltpu.VMEM((slots, cx + 2, cy + 2 * PAD, cz), jnp.float32)
     dma = pltpu.SemaphoreType.DMA
     any_space = pl.BlockSpec(memory_space=pl.ANY)
-    scalars = pl.BlockSpec(memory_space=pltpu.SMEM)
+    in_hbm = pl.BlockSpec(memory_space=pltpu.HBM)
     return pl.pallas_call(
         functools.partial(kernel, sizes),
         out_shape=jax.ShapeDtypeStruct(phase.shape, jnp.float32),
-        in_specs=[any_space] + [scalars] * 5,
+        in_specs=[in_hbm] * 6,
         out_specs=any_space,
         scratch_shapes=[
+            pltpu.SMEM(slot_grain.shape, jnp.int32), pltpu.SMEM(crowding.shape, jnp.int32),
+            pltpu.SMEM(grain_home.shape, jnp.int32), pltpu.SMEM(grain_weight.shape, jnp.float32),
+            pltpu.SMEM(grain_target.shape, jnp.float32),
             field, field,
             pltpu.VMEM((tiles, 2, 8, cz), jnp.float32),
             pltpu.VMEM((8, cz), jnp.int32),
             pltpu.SMEM((8, cz), jnp.int32),
-            pltpu.VMEM((4, slots, 8, cz), jnp.float32),
+            pltpu.VMEM((5, slots, 8, cz), jnp.float32),
             [pltpu.VMEM((slots + 1, cy // CHUNKS, cz), jnp.float32)] * (4 * CHUNKS),
             [pltpu.VMEM((slots + 1, cx, 8, cz), jnp.float32)] * 4,
             [pltpu.VMEM((slots + 1, 8, cz), jnp.float32)] * 2,
             [pltpu.VMEM((slots, 8, cz), jnp.float32)] * 2,
-            dma((slots,)), dma((tiles,)), dma((tiles,)), dma,
+            dma((5,)), dma((slots,)), dma((tiles,)), dma((tiles,)), dma,
             dma((4 * CHUNKS,)), dma((4 * CHUNKS,)), dma((4,)), dma((4,)),
             dma((2,)), dma((2,)), dma((3 * CHUNKS,)),
         ],
         compiler_params=pltpu.CompilerParams(
-            collective_id=0, has_side_effects=True, vmem_limit_bytes=40 * 2**20
+            collective_id=0, has_side_effects=True, vmem_limit_bytes=62 * 2**20
         ),
     )(phase, slot_grain, crowding, grain_home, grain_weight, grain_target)
 

time: 42.3 us -> 33.9 us (0.80)
  Pallas kernels: 36 us -> 29.9 us
  local copies, waits for them, and re-layouts: 5.52 us -> 3.16 us
    pallas_call x1, Pallas kernels: 36 us -> 29.9 us  [on_device(): pl.pallas_call(functools.partial(kernel, sizes), out_shape=jax.ShapeDtype...]
    unnamed x11 -> x1, local copies, waits for them, and re-layouts: 5.52 us -> 3.16 us
where the time goes in v2:
time: 33.9 us; the launch traced here: 33.7 us
  Pallas kernels  29.9 us (88%)
  local copies, waits for them, and re-layouts  3.16 us (9%)
  between operations  0.66 us (2%)
    pallas_call x1, Pallas kernels, on_device(): pl.pallas_call(functools.partial(kernel, sizes), out_shape=jax.ShapeDtype...  29.9 us
    unnamed x1, local copies, waits for them, and re-layouts  3.16 us

profile of v2, /device:TPU:0, one launch (start us, length us, event | category | flops | bytes accessed | tf_op | source)
XLA Modules:
  0.0 33.7 jit_solution(2871496320641233918)
XLA Ops:
  0.7 29.9 %shard_map.64 = f32[8,8,64,128]{3,2,1,0:T(8,128)} custom-call(f32[8,8,64,128]{3,2,1,0:T(8,128)} %phase.1, s32[1,1,1,8]{3,2,1,0:T(1,128)} %grain_in.1, s32[1,1,1]{2,1,0:T(1,128)S(6)} %copy.8.crowd_in, s32[64]{0:T(128)} %home_in.1, f32[64]{0:T(128)} %weight_in.1, f32[64]{0:T(128)} %target_in.1), custom_call_target="tpu_custom_call" | custom-call | tf_op jit(solution)/shard_map/pallas_call | solution.py:317
  30.6 3.2 %copy.9 = f32[8,8,64,128]{3,2,1,0:T(8,128)} copy(f32[8,8,64,128]{3,2,1,0:T(8,128)} %shard_map.64) | data formatting | bytes 4194304

commit v3 on v2

--- a/solution.py
+++ b/solution.py
@@ -22,8 +22,8 @@
 
 def kernel(
     sizes, phase, grain_in, crowd_in, home_in, weight_in, target_in, out,
-    grain, crowd, home, weight, target, first, second, msg, places, place, coef, xin, yin, zin, zout,
-    small_sem, load_sem, msg_send, msg_recv, place_sem, x_send, x_recv, y_send, y_recv,
+    grain, crowd, home, weight, target, first, second, nearby, msg, ids_of, places, place, coef, xin, yin, zin, zout,
+    small_sem, load_sem, ids_send, ids_recv, msg_send, msg_recv, place_sem, x_send, x_recv, y_send, y_recv,
     z_send, z_recv, out_sem,
 ):
     tiles_x, tiles_y, tiles_z = sizes
@@ -85,7 +85,7 @@
     for s in range(slots):
         id_rows = jnp.where(row == s, ids[s], id_rows)
         mine_lanes = jnp.where(lane == s, mine[s], mine_lanes)
-    msg[0, 1] = id_rows
+    ids_of[0] = id_rows
 
     pl.semaphore_wait(barrier, tiles - 1)
 
@@ -131,6 +131,13 @@
         for side in range(2):
             pl.when(goes[side][1])(lambda: y_copy(step, side).start())
 
+    def ids_copy(k):
+        return pltpu.make_async_remote_copy(
+            ids_of.at[0], ids_of.at[k], ids_send.at[k], ids_recv.at[k],
+            device_id=partner(k), device_id_type=MESH,
+        )
+
+    each(1, tiles, lambda k: ids_copy(k).start())
     send_y(0)
     send_x(0, 0)
 
@@ -140,7 +147,7 @@
         while len(parts) > 1:
             parts = [a + b for a, b in zip(parts[::2], parts[1::2])]
         total = jnp.where(live[s], jnp.sum(parts[0], axis=0, keepdims=True), 0.0)
-        msg[0, 0, s:s + 1] = total
+        msg[0, s:s + 1] = total
 
     def msg_copy(k):
         return pltpu.make_async_remote_copy(
@@ -164,14 +171,14 @@
                     parts.append(pltpu.roll(part, 2 * k, 1) if k else part)
             while len(parts) > 1:
                 parts = [a + b for a, b in zip(parts[::2], parts[1::2])]
-            zout[step][s] = parts[0]
+            zout[step][s] = pltpu.roll(parts[0], 1 - tz, 1)
 
         z_copy(step).start()
 
     pack_z(0, first)
-    for c in range(1, CHUNKS):
+    for c in [CHUNKS - 1] + list(range(1, CHUNKS - 1)):
         send_x(0, c)
-    each(1, tiles, lambda k: msg_copy(k).wait_recv())
+    each(1, tiles, lambda k: ids_copy(k).wait_recv())
 
     plane = tiles_y * tiles_z
     froms = (
@@ -181,15 +188,93 @@
     )
     table = jnp.zeros((8, cz), jnp.int32)
     for f, (k, there) in enumerate(froms):
-        same = (msg[k % tiles, 1] == mine_lanes) & there
+        same = (ids_of[k % tiles] == mine_lanes) & there
         found = jnp.max(jnp.where(same, slots - row, 0), axis=0, keepdims=True)
         table = jnp.where(row == f, slots - found, table)
     places[...] = table
     to_scalars = pltpu.make_async_copy(places, place, place_sem)
     to_scalars.start()
 
+    to_scalars.wait()
+
+    low_lane, high_lane = lane == 0, lane == cz - 1
+    from_high = jnp.where(tz == 0, 1.0, 0.0).astype(jnp.float32)
+    from_low = 1.0 - from_high
+
+    def tree(parts):
+        while len(parts) > 1:
+            parts = [a + b for a, b in zip(parts[::2], parts[1::2])] + parts[len(parts) // 2 * 2:]
+        return parts[0]
+
+    def take_yz(step, src):
+        z_copy(step).wait_recv()
+        for side in range(2):
+            pl.when(comes[side][1])(lambda: y_copy(step, side).wait_recv())
+        for side in range(2):
+            for s in range(slots):
+                ghost_row = (PAD - 1, PAD + cy)[side]
+                src[s, pl.ds(1, cx), pl.ds(ghost_row, 1)] = yin[step * 2 + side][
+                    place[2 + side, s], :, pl.ds(0, 1)
+                ]
+
+    def sum_nearby(step, src):
+        @pl.loop(0, slots)
+        def _(s):
+            face = zin[step][jnp.where(tz == 0, place[4, s], place[5, s])]
+            for x in range(cx):
+                for t in range(cy // 8):
+                    start = PAD + 8 * t
+                    p = src[s, x + 1, pl.ds(start, 8)]
+                    k = x + cx * t
+                    ghost = jnp.broadcast_to(face[:, 2 * k:2 * k + 1], (8, cz))
+                    near = [
+                        pltpu.roll(jnp.where(low_lane, ghost * from_high, p), cz - 1, 1),
+                        pltpu.roll(jnp.where(high_lane, ghost * from_low, p), 1, 1),
+                        src[s, x + 1, pl.ds(start - 1, 8)],
+                        src[s, x + 1, pl.ds(start + 1, 8)],
+                    ]
+                    if x > 0:
+                        near.append(src[s, x, pl.ds(start, 8)])
+                    if x < cx - 1:
+                        near.append(src[s, x + 2, pl.ds(start, 8)])
+                    nearby[s, x, pl.ds(8 * t, 8)] = tree(near)
+
+    def advance(step, src, dst, c, x, side=None):
+        for t in range(rows // 8):
+            start = c * rows + 8 * t
+            squares = []
+            for s in range(slots):
+                p = src[s, x, pl.ds(PAD + start, 8)]
+                squares.append(coef[2, s] * (p * p))
+            mixed = tree(squares)
+            updates = []
+            for s in range(slots):
+                p = src[s, x, pl.ds(PAD + start, 8)]
+                beside = nearby[s, x - 1, pl.ds(start, 8)]
+                if side is not None:
+                    face = xin[(step * 2 + side) * CHUNKS + c]
+                    beside = beside + face[place[side, s], pl.ds(8 * t, 8)]
+                slope = coef[0, s] - coef[1, s] * p - coef[3, s] * (mixed - squares[s])
+                updates.append(jnp.maximum(coef[4, s] * beside + p * slope, 0.0))
+            scale = 1.0 / jnp.maximum(tree(updates), 1.0)
+            for s in range(slots):
+                dst[s, x, pl.ds(PAD + start, 8)] = updates[s] * scale
+
+    def edges(step, src, dst, c):
+        for side in range(2):
+            pl.when(comes[side][0])(lambda: x_copy(step, side, c).wait_recv())
+        for side in range(2):
+            advance(step, src, dst, c, (1, cx)[side], side)
+
+    def inner_layers(step, src, dst, c):
+        pl.loop(2, cx)(lambda x: advance(step, src, dst, c, x))
+
+    take_yz(0, first)
+    sum_nearby(0, first)
+    each(1, tiles, lambda k: msg_copy(k).wait_recv())
+
     def add_tile(k, sums):
-        ids_k, sums_k = msg[k, 1], msg[k, 0]
+        ids_k, sums_k = ids_of[k], msg[k]
         return tuple(
             sums[s] + jnp.where(ids_k == mine[s], sums_k, 0.0) for s in range(slots)
         )
@@ -208,95 +293,38 @@
         coef[2, s] = jnp.full((8, cz), w, jnp.float32)
         coef[3, s] = jnp.full((8, cz), 0.4 * w, jnp.float32)
         coef[4, s] = jnp.full((8, cz), jnp.where(live[s], 0.1, 0.0), jnp.float32)
-    to_scalars.wait()
-    z_place = [jnp.where(tz == 0, place[4, s], place[5, s]) for s in range(slots)]
-
-    low_lane, high_lane = lane == 0, lane == cz - 1
-
-    def advance(step, src, dst, c, x):
-        for t in range(rows // 8):
-            advance_rows(step, src, dst, c * (rows // 8) + t, x)
-
-    def advance_rows(step, src, dst, t, x):
-        start = PAD + 8 * t
-        faces = zin[step]
-        turn = lax.rem(2 * cz - 2 * ((x - 1) + cx * t), cz)
-        squares, mixed = [], jnp.zeros((8, cz), jnp.float32)
-        for s in range(slots):
-            p = src[s, x, pl.ds(start, 8)]
-            square = coef[2, s] * (p * p)
-            mixed = mixed + square
-            squares.append(square)
-        total = jnp.zeros((8, cz), jnp.float32)
-        updates = []
-        for s in range(slots):
-            p = src[s, x, pl.ds(start, 8)]
-            ghost = pltpu.roll(faces[z_place[s]], turn, 1)
-            beside = pltpu.roll(jnp.where(low_lane, ghost, p), cz - 1, 1)
-            beside = beside + pltpu.roll(jnp.where(high_lane, ghost, p), 1, 1)
-            beside = beside + (src[s, x, pl.ds(start - 1, 8)] + src[s, x, pl.ds(start + 1, 8)])
-            beside = beside + (src[s, x - 1, pl.ds(start, 8)] + src[s, x + 1, pl.ds(start, 8)])
-            slope = coef[0, s] - coef[1, s] * p - coef[3, s] * (mixed - squares[s])
-            update = jnp.maximum(coef[4, s] * beside + p * slope, 0.0)
-            total = total + update
-            updates.append(update)
-        scale = 1.0 / jnp.maximum(total, 1.0)
-        for s in range(slots):
-            dst[s, x, pl.ds(start, 8)] = updates[s] * scale
-
-    def take_yz(step, src):
-        z_copy(step).wait_recv()
-        for side in range(2):
-            pl.when(comes[side][1])(lambda: y_copy(step, side).wait_recv())
-        for side in range(2):
-            for s in range(slots):
-                ghost_row = (PAD - 1, PAD + cy)[side]
-                src[s, pl.ds(1, cx), pl.ds(ghost_row, 1)] = yin[step * 2 + side][
-                    place[2 + side, s], :, pl.ds(0, 1)
-                ]
-
-    def take_x(step, src, c):
-        for side in range(2):
-            pl.when(comes[side][0])(lambda: x_copy(step, side, c).wait_recv())
-            for s in range(slots):
-                src[s, (0, cx + 1)[side], pl.ds(PAD + c * rows, rows)] = xin[
-                    (step * 2 + side) * CHUNKS + c
-                ][place[side, s]]
-
-    take_yz(0, first)
-    for c in range(CHUNKS):
-        take_x(0, first, c)
-        pl.loop(0, 2)(lambda i: advance(0, first, second, c, 1 + i * (cx - 1)))
+    order = [0, CHUNKS - 1] + list(range(1, CHUNKS - 1))
+    for i, c in enumerate(order):
+        edges(0, first, second, c)
         send_x(1, c)
-        pl.loop(2, cx)(lambda x: advance(0, first, second, c, x))
-    send_y(1)
+        inner_layers(0, first, second, c)
+        if i == 1:
+            send_y(1)
     pack_z(1, second)
 
-    def out_copy(i, x, start, count):
-        return pltpu.make_async_copy(
-            first.at[:, x, pl.ds(PAD + start, count)],
-            out.at[:, x - 1, pl.ds(start, count)], out_sem.at[i],
-        )
-
     take_yz(1, second)
+    sum_nearby(1, second)
     outs = []
-    for c in range(CHUNKS):
-        pl.loop(2, cx)(lambda x: advance(1, second, first, c, x))
+
+    def put(layers, c):
+        low, count = layers
         copy = pltpu.make_async_copy(
-            first.at[:, pl.ds(2, cx - 2), pl.ds(PAD + c * rows, rows)],
-            out.at[:, pl.ds(1, cx - 2), pl.ds(c * rows, rows)], out_sem.at[c],
+            first.at[:, pl.ds(low + 1, count), pl.ds(PAD + c * rows, rows)],
+            out.at[:, pl.ds(low, count), pl.ds(c * rows, rows)], out_sem.at[len(outs)],
         )
         copy.start()
         outs.append(copy)
-    for c in range(CHUNKS):
-        take_x(1, second, c)
-        pl.loop(0, 2)(lambda i: advance(1, second, first, c, 1 + i * (cx - 1)))
-        for i, x in enumerate((1, cx)):
-            copy = out_copy(CHUNKS * (1 + i) + c, x, c * rows, rows)
-            copy.start()
-            outs.append(copy)
+
+    for c in order:
+        inner_layers(1, second, first, c)
+        put((1, cx - 2), c)
+    for c in order:
+        edges(1, second, first, c)
+        put((0, 1), c)
+        put((cx - 1, 1), c)
 
     each(1, tiles, lambda k: msg_copy(k).wait_send())
+    each(1, tiles, lambda k: ids_copy(k).wait_send())
     for step in range(2):
         z_copy(step).wait_send()
         for side in range(2):
@@ -324,7 +352,9 @@
             pltpu.SMEM(grain_home.shape, jnp.int32), pltpu.SMEM(grain_weight.shape, jnp.float32),
             pltpu.SMEM(grain_target.shape, jnp.float32),
             field, field,
-            pltpu.VMEM((tiles, 2, 8, cz), jnp.float32),
+            pltpu.VMEM((slots, cx, cy, cz), jnp.float32),
+            pltpu.VMEM((tiles, 8, cz), jnp.float32),
+            pltpu.VMEM((tiles, 8, cz), jnp.float32),
             pltpu.VMEM((8, cz), jnp.int32),
             pltpu.SMEM((8, cz), jnp.int32),
             pltpu.VMEM((5, slots, 8, cz), jnp.float32),
@@ -332,7 +362,7 @@
             [pltpu.VMEM((slots + 1, cx, 8, cz), jnp.float32)] * 4,
             [pltpu.VMEM((slots + 1, 8, cz), jnp.float32)] * 2,
             [pltpu.VMEM((slots, 8, cz), jnp.float32)] * 2,
-            dma((5,)), dma((slots,)), dma((tiles,)), dma((tiles,)), dma,
+            dma((5,)), dma((slots,)), dma((tiles,)), dma((tiles,)), dma((tiles,)), dma((tiles,)), dma,
             dma((4 * CHUNKS,)), dma((4 * CHUNKS,)), dma((4,)), dma((4,)),
             dma((2,)), dma((2,)), dma((3 * CHUNKS,)),
         ],

time: 33.9 us -> 29.5 us (0.87); the launches traced: 33.7 us -> 29 us
  Pallas kernels: 29.9 us -> 25.2 us
    pallas_call x1, Pallas kernels: 29.9 us -> 25.2 us  [on_device(): pl.pallas_call(functools.partial(kernel, sizes), out_shape=jax.ShapeDtype...]
where the time goes in v3:
time: 29.5 us; the launch traced here: 29 us
  Pallas kernels  25.2 us (85%)
  local copies, waits for them, and re-layouts  3.16 us (11%)
  between operations  0.66 us (2%)
    pallas_call x1, Pallas kernels, on_device(): pl.pallas_call(functools.partial(kernel, sizes), out_shape=jax.ShapeDtype...  25.2 us
    unnamed x1, local copies, waits for them, and re-layouts  3.16 us

profile of v3, /device:TPU:0, one launch (start us, length us, event | category | flops | bytes accessed | tf_op | source)
XLA Modules:
  0.0 29.0 jit_solution(5767205249262767567)
XLA Ops:
  0.7 25.2 %shard_map.64 = f32[8,8,64,128]{3,2,1,0:T(8,128)} custom-call(f32[8,8,64,128]{3,2,1,0:T(8,128)} %phase.1, s32[1,1,1,8]{3,2,1,0:T(1,128)} %grain_in.1, s32[1,1,1]{2,1,0:T(1,128)S(6)} %copy.8.crowd_in, s32[64]{0:T(128)} %home_in.1, f32[64]{0:T(128)} %weight_in.1, f32[64]{0:T(128)} %target_in.1), custom_call_target="tpu_custom_call" | custom-call | tf_op jit(solution)/shard_map/pallas_call | solution.py:345
  25.8 3.2 %copy.9 = f32[8,8,64,128]{3,2,1,0:T(8,128)} copy(f32[8,8,64,128]{3,2,1,0:T(8,128)} %shard_map.64) | data formatting | bytes 4194304
